TPU v7x, 32 devices: a whole 2x2x4 slice. The times are simulated.
32 devices in a mesh: groups: 2 (over x), seq: 16 (over z, y, core).
Axes of the slice: x: 2, y: 2, z: 4, core: 2. Of those that a mesh axis runs over, the one named last changes fastest.
Arguments:
- mixer_in: bfloat16 [2048, 4608], P(('groups', 'seq')), parts along dimension 0, may hold values from -6 to 6
- gate_in: bfloat16 [2048, 4096], P(('groups', 'seq')), parts along dimension 0, may hold values from -6 to 6
- step_raw: bfloat16 [2048, 64], P(('groups', 'seq')), parts along dimension 0, may hold values from -3 to 3
- step_bias: float32 [64], replicated, may hold values from -1.5 to 0
- rate_log: float32 [64], replicated, as said below
- conv_weight: float32 [4, 4608], replicated, may hold values from -3 to 3
- conv_bias: float32 [4608], replicated, may hold values from -0.5 to 0.5
- skip_gain: float32 [64], replicated, may hold values from 0.5 to 1.5
- norm_gain: float32 [4096], replicated, may hold values from 0.1 to 1.9
- doc_lengths: int32 [12], P('groups'), parts along dimension 0, may hold values from 1 to 512, 1024 in all
Outputs:
- mixed_out: bfloat16 [2048, 4096], P(('groups', 'seq')), parts along dimension 0
There are 2 independent parts, one for each index of `groups`. A program takes and returns all parts, laid end to end along the dimension named above; an argument that names none is the same for every part. Nothing has to cross between parts.
Inputs may be any that keep to these rules, and one draw needn't show every extreme that they name: `doc_lengths`: the 6 lengths of a part sum to 1024, and the longest is exactly 512. exp(rate_log) lies between 0.3 / 1024 and 0.08.
All inputs are finite; a program needn't handle non-finite values.
Results may differ from a plain program's by a relative error of at most 0.0043.
Values may be sent and summed in bfloat16 or wider, within the bound.
A program may use at most 320 MiB of HBM per device.

v0:
```python
import jax
import jax.numpy as jnp
from jax import lax
from jax.sharding import PartitionSpec as P

GROUPS = 4


epsilon = 1e-05


def from_behind(block, axis, distance):
    devices = range(lax.axis_size(axis))
    route = [(i - distance, i) for i in devices if i - distance in devices]
    return lax.ppermute(block, axis, route)


def doc_index(doc_lengths, positions):
    doc_ends = jnp.cumsum(doc_lengths)
    inside = jnp.sum((positions[:, None] >= doc_ends[None, :]).astype(jnp.int32), axis=1)
    return jnp.where(positions >= 0, inside, -1)


def convolve(tok_block, rim_rows, positions, doc_lengths, conv_weight, conv_bias):
    rim_width = rim_rows.shape[0]
    length = tok_block.shape[0]
    padded = jnp.concatenate([rim_rows, tok_block], axis=0).astype(jnp.float32)
    all_positions = jnp.concatenate([positions[:rim_width] - rim_width, positions])
    doc_ids = doc_index(doc_lengths, all_positions)
    own_doc = doc_ids[rim_width:]
    summed = jnp.zeros(tok_block.shape, jnp.float32) + conv_bias[None, :]
    for offset in range(rim_width + 1):
        same_doc = (doc_ids[offset : offset + length] == own_doc)[:, None]
        summed = summed + conv_weight[offset][None, :] * jnp.where(
            same_doc, padded[offset : offset + length], 0.0
        )
    return (jax.nn.silu(summed).astype(jnp.bfloat16), own_doc, doc_ids[rim_width - 1])


def group_terms(
    conv_x,
    conv_b,
    conv_c,
    step_size,
    log_sums,
    own_doc,
    prior_doc,
    skip_gain,
    member,
    group_heads,
    state_size,
):
    length = conv_x.shape[0]
    head_size = conv_x.shape[1] // skip_gain.shape[0]
    first = member * group_heads
    picked = slice(first, first + group_heads)
    x_group = conv_x[:, first * head_size : (first + group_heads) * head_size].reshape(
        length, group_heads, head_size
    )
    b_group = conv_b[:, member * state_size : (member + 1) * state_size]
    c_group = conv_c[:, member * state_size : (member + 1) * state_size]
    scores = jnp.einsum("tn,sn->ts", c_group, b_group, preferred_element_type=jnp.float32)
    places = jnp.arange(length, dtype=jnp.int32)
    causal = (places[:, None] >= places[None, :]) & (own_doc[:, None] == own_doc[None, :])
    head_logs = log_sums[:, picked].T
    log_gaps = head_logs[:, :, None] - head_logs[:, None, :]
    decays = jnp.exp(jnp.where(causal[None], log_gaps, -jnp.inf))
    head_steps = step_size[:, picked].T
    weights = (decays * scores[None] * head_steps[:, None, :]).astype(jnp.bfloat16)
    within = jnp.einsum("hts,shp->thp", weights, x_group, preferred_element_type=jnp.float32)
    within = within + skip_gain[picked][None, :, None] * x_group.astype(jnp.float32)
    final_log = log_sums[-1, picked]
    tail_scale = (
        jnp.exp(final_log[None, :] - log_sums[:, picked])
        * step_size[:, picked]
        * (own_doc == own_doc[-1]).astype(jnp.float32)[:, None]
    )
    weighted = (x_group * tail_scale[:, :, None]).astype(jnp.bfloat16)
    local_state = jnp.einsum("shp,sn->hpn", weighted, b_group, preferred_element_type=jnp.float32)
    inward = jnp.exp(log_sums[:, picked]) * (own_doc == prior_doc).astype(jnp.float32)[:, None]
    passing = jnp.exp(final_log) * (own_doc[-1] == prior_doc).astype(jnp.float32)
    return (within, local_state, inward, passing)


def carry_term(c_group, state_in, inward):
    rounded = state_in.astype(jnp.bfloat16)
    term = jnp.einsum("tn,hpn->thp", c_group, rounded, preferred_element_type=jnp.float32)
    return term * inward[:, :, None]


def finish(mixed_out, gate_rows, norm_gain):
    length, head_count, head_size = mixed_out.shape
    gated = mixed_out * jax.nn.silu(gate_rows.astype(jnp.float32)).reshape(
        length, head_count, head_size
    )
    inv_rms = lax.rsqrt(jnp.mean(gated * gated, axis=2, keepdims=True) + epsilon)
    return ((gated * inv_rms).reshape(length, head_count * head_size) * norm_gain[None, :]).astype(
        jnp.bfloat16
    )


def linked(earlier, later):
    return (earlier[0] * later[0], later[0][..., None] * earlier[1] + later[1])


def on_device(
    mixer_in,
    gate_in,
    step_raw,
    step_bias,
    rate_log,
    conv_weight,
    conv_bias,
    skip_gain,
    norm_gain,
    doc_lengths,
):
    tok_rows = mixer_in.shape[0]
    rim_width = conv_weight.shape[0] - 1
    head_count = rate_log.shape[0]
    inner_width = gate_in.shape[1]
    head_width = inner_width // head_count
    state_size = (mixer_in.shape[1] - inner_width) // (2 * GROUPS)
    group_heads = head_count // GROUPS
    rim_rows = from_behind(mixer_in[tok_rows - rim_width :], "seq", 1)
    positions = lax.axis_index("seq") * tok_rows + jnp.arange(tok_rows, dtype=jnp.int32)
    mixed, own_doc, prior_doc = convolve(
        mixer_in, rim_rows, positions, doc_lengths, conv_weight, conv_bias
    )
    conv_x = mixed[:, :inner_width]
    conv_b = mixed[:, inner_width : inner_width + GROUPS * state_size]
    conv_c = mixed[:, inner_width + GROUPS * state_size :]
    step_size = jax.nn.softplus(step_raw.astype(jnp.float32) + step_bias[None, :])
    log_sums = jnp.cumsum(-jnp.exp(rate_log)[None, :] * step_size, axis=0)
    pieces = [
        group_terms(
            conv_x,
            conv_b,
            conv_c,
            step_size,
            log_sums,
            own_doc,
            prior_doc,
            skip_gain,
            member,
            group_heads,
            state_size,
        )
        for member in range(GROUPS)
    ]
    passings = jnp.concatenate([piece_set[3] for piece_set in pieces], axis=0)
    local_states = jnp.concatenate([piece_set[1] for piece_set in pieces], axis=0)
    row_count = head_count * head_width
    row_pass = jnp.repeat(passings, head_width)[None, :]
    row_states = local_states.reshape(1, row_count, state_size)
    block_states, block_pass = (
        lax.all_to_all(row_states, "seq", split_axis=1, concat_axis=0, tiled=True),
        lax.all_to_all(row_pass, "seq", split_axis=1, concat_axis=0, tiled=True),
    )
    inclusive = lax.associative_scan(linked, (block_pass, block_states), axis=0)
    exclusive = jnp.concatenate([jnp.zeros_like(block_states[:1]), inclusive[1][:-1]], axis=0)
    returned = lax.all_to_all(
        exclusive.astype(jnp.bfloat16), "seq", split_axis=0, concat_axis=1, tiled=True
    ).astype(exclusive.dtype)
    whole_state = returned.reshape(head_count, head_width, state_size)
    arrivals = [
        whole_state[member * group_heads : (member + 1) * group_heads] for member in range(GROUPS)
    ]
    results = []
    for member in range(GROUPS):
        c_group = conv_c[:, member * state_size : (member + 1) * state_size]
        results.append(pieces[member][0] + carry_term(c_group, arrivals[member], pieces[member][2]))
    mixed_out = jnp.concatenate(results, axis=1)
    return finish(mixed_out, gate_in, norm_gain)


def solution(mesh):
    return jax.shard_map(
        on_device,
        mesh=mesh,
        in_specs=(
            P(("groups", "seq"), None),
            P(("groups", "seq"), None),
            P(("groups", "seq"), None),
            P(),
            P(),
            P(),
            P(),
            P(),
            P(),
            P("groups"),
        ),
        out_specs=P(("groups", "seq"), None),
        check_vma=False,
    )
```

profile of v0, /device:TPU:0, one launch (start us, length us, event | category | flops | bytes accessed | tf_op | source)
XLA Modules:
  0.0 141.5 jit_solution(8743664559068083938)
XLA Ops:
  0.0 1.0 slice.290
  1.0 2.4 %collective-permute-start = (bf16[3,4608]{1,0:T(4,128)(2,1)S(1)}, bf16[3,4608]{1,0:T(4,128)(2,1)S(1)}, u32[]{:S(2)}, u32[]{:S(2)}) collective-permute-start(bf16[3,4608]{1,0:T(4,128)(2,1)S(1)} %slice.290), channel_id=1, source_target_pairs={{0,1},{1,2},{2,3},{3,4},{4,5},{5,6},{6,7},{7,8},{8,9},{9,10},{10,1... | collective-permute-start | bytes 82952 | tf_op jit(solution)/shard_map/ppermute | solution.py:15
  3.5 0.8 reduce-window.8
  5.1 0.8 copy.154
  6.5 0.8 compare_select_fusion
  9.3 0.7 broadcast_in_dim.68
  10.0 7.2 %all-to-all-start.1 = ((f32[1,16,256]{2,0,1:T(1,128)}), f32[1,16,256]{2,0,1:T(1,128)S(1)}, u32[]{:S(2)}, u32[]{:S(2)}) async-start(f32[1,16,256]{2,0,1:T(1,128)} %broadcast_in_dim.68), calls=%async_computation.1 | async-start | bytes 32768 | tf_op jit(solution)/shard_map/all_to_all | solution.py:158
  17.2 1.3 compare_convert_fusion
  19.6 1.2 slice_reduce_fusion.3
  21.0 1.1 multiply_convert_fusion
  24.7 19.3 %reduce.24 = f32[4096,64]{1,0:T(8,128)} reduce(f32[4096,1,64]{2,1,0:T(1,128)S(1)} %bitcast.110, f32[]{:T(128)} %broadcast.143), dimensions={1}, to_apply=%bitcast.95.reduce_sub_computation | reduce | bytes 2097156
  44.0 3.4 %reshape.249 = f32[16,1,16384]{2,1,0:T(1,128)} reshape(f32[4096,64]{1,0:T(8,128)} %reduce.24) | data formatting | bytes 2097152
  47.5 6.1 %all-to-all-start = ((f32[16,1,16384]{2,1,0:T(1,128)}), f32[16,1,16384]{2,1,0:T(1,128)S(1)}, u32[]{:S(2)}, u32[]{:S(2)}) async-start(f32[16,1,16384]{2,1,0:T(1,128)} %reshape.249), calls=%async_computation | async-start | bytes 2097152 | tf_op jit(solution)/shard_map/all_to_all | solution.py:157
  54.4 1.3 convert_multiply_fusion
  57.5 19.0 %all-to-all-done = f32[16,1,16384]{2,1,0:T(1,128)S(1)} async-done(((f32[16,1,16384]{2,1,0:T(1,128)}), f32[16,1,16384]{2,1,0:T(1,128)S(1)}, u32[]{:S(2)}, u32[]{:S(2)}) %all-to-all-start) | async-done | bytes 1048608 | tf_op jit(solution)/shard_map/all_to_all | solution.py:157
  76.6 3.1 %reduce.25 = f32[16,16384]{1,0:T(8,128)S(1)} reduce(f32[16,1,16384]{2,1,0:T(1,128)S(1)} %all-to-all-done, f32[]{:T(128)} %broadcast.143), dimensions={1}, to_apply=%all_to_all.13.reduce_sub_computation | reduce | bytes 2097156 | tf_op jit(solution)/shard_map/all_to_all | solution.py:157
  79.7 2.6 %reshape.250 = f32[4096,1,64]{2,1,0:T(1,128)S(1)} reshape(f32[16,16384]{1,0:T(8,128)S(1)} %reduce.25) | data formatting | bytes 2097152
  82.3 1.0 slice.351
  83.3 1.1 fusion.96
  84.4 2.3 %copy.183 = f32[8,256,64]{1,2,0:T(8,128)} copy(f32[8,256,64]{2,1,0:T(8,128)} %get-tuple-element.16) | data formatting | bytes 1048576
  86.8 1.1 copy.182
  87.9 1.4 multiply_add_fusion
  89.3 0.7 slice_add_fusion
  90.6 1.1 copy.184
  91.7 1.0 slice_add_fusion.1
  92.8 0.9 fusion.99
  94.5 0.7 add.148
  95.2 1.8 %pad.32 = f32[8,256,64]{1,2,0:T(8,128)S(1)} pad(f32[4,256,64]{1,2,0:T(8,128)} %add.148, f32[]{:T(128)} %constant.34.clone.1), padding=1_0_1x0_0_0x0_0_0 | pad | bytes 786436 | tf_op jit(solution)/shard_map/pad | solution.py:160
  97.0 1.0 fusion.59
  98.2 0.9 add.150
  99.4 0.9 copy-done.4
  100.6 0.8 concatenate.37
  101.4 6.9 %all-to-all-start.2 = ((bf16[16,256,64]{1,2,0:T(8,128)(2,1)}), bf16[16,256,64]{1,2,0:T(8,128)(2,1)}, u32[]{:S(2)}, u32[]{:S(2)}) async-start(bf16[16,256,64]{1,2,0:T(8,128)(2,1)} %concatenate.37), calls=%async_computation.2 | async-start | bytes 1048576 | tf_op jit(solution)/shard_map/all_to_all | solution.py:162
  109.6 1.6 %fusion.73 = f32[64,64]{1,0:T(8,128)} fusion(bf16[64,4608]{1,0:T(8,128)(2,1)} %copy-done.3), kind=kOutput, calls=%fused_computation.123 | convolution fusion | flops 524288 | bytes 49152 | tf_op jit(solution)/shard_map/tn,sn->ts/dot_general | solution.py:62
  111.1 1.5 %fusion.76 = f32[64,64]{1,0:T(8,128)} fusion(bf16[64,4608]{1,0:T(8,128)(2,1)} %copy-done.3), kind=kOutput, calls=%fused_computation.126 | convolution fusion | flops 524288 | bytes 49152 | tf_op jit(solution)/shard_map/tn,sn->ts/dot_general | solution.py:62
  112.6 1.5 %fusion.79 = f32[64,64]{1,0:T(8,128)} fusion(bf16[64,4608]{1,0:T(8,128)(2,1)} %copy-done.3), kind=kOutput, calls=%fused_computation.129 | convolution fusion | flops 524288 | bytes 49152 | tf_op jit(solution)/shard_map/tn,sn->ts/dot_general | solution.py:62
  114.2 1.5 %fusion.88 = f32[64,64]{1,0:T(8,128)} fusion(bf16[64,4608]{1,0:T(8,128)(2,1)} %copy-done.3), kind=kOutput, calls=%fused_computation.138 | convolution fusion | flops 524288 | bytes 49152 | tf_op jit(solution)/shard_map/tn,sn->ts/dot_general | solution.py:62
  115.6 7.2 %all-to-all-done.2 = bf16[16,256,64]{1,2,0:T(8,128)(2,1)} async-done(((bf16[16,256,64]{1,2,0:T(8,128)(2,1)}), bf16[16,256,64]{1,2,0:T(8,128)(2,1)}, u32[]{:S(2)}, u32[]{:S(2)}) %all-to-all-start.2) | async-done | bytes 524320 | tf_op jit(solution)/shard_map/all_to_all | solution.py:162
  122.9 1.3 copy.168
  125.2 1.0 convolution_multiply_fusion
  126.3 1.0 convolution_multiply_fusion.1
  127.4 1.0 convolution_multiply_fusion.2
  128.4 0.9 convolution_multiply_fusion.3
  131.2 1.9 %pad_maximum_fusion.1 = (f32[64,64,64]{0,2,1:T(8,128)}, f32[64,64]{0,1:T(8,128)S(1)}) fusion(f32[64,16,64]{0,2,1:T(8,128)S(1)} %fusion.7, f32[64,16,64]{0,2,1:T(8,128)S(1)} %fusion.5, f32[64,16,64]{0,2,1:T(8,128)S(1)} %fusion.3, f32[64,16,64]{0,2,1:T(8,128)S(1)} %fusion.1, f32[64,4096]{0,1:T(8,128)S(1)} %copy.174), kind=kLoop, calls=%fused_computation.1 | loop fusion | flops 1568768 | bytes 3162112 | tf_op jit(solution)/shard_map/concatenate | solution.py:173
  133.2 1.9 %mul.516 = f32[64,64,64]{2,1,0:T(8,128)} broadcast(f32[64,64]{1,0:T(8,128)S(1)} %copy.175), dimensions={0,1} | broadcast | bytes 1064960 | tf_op jit(solution)/shard_map/mul | solution.py:97
  135.1 2.3 %mul.517 = f32[64,4096]{1,0:T(8,128)S(1)} reshape(f32[64,64,64]{2,1,0:T(8,128)} %mul.516) | data formatting | bytes 2097152 | tf_op jit(solution)/shard_map/mul | solution.py:97
  137.4 1.6 %copy.173 = f32[64,4096]{1,0:T(8,128)} copy(f32[64,4096]{0,1:T(8,128)S(1)} %bitcast.109) | data formatting | bytes 2097152 | tf_op jit(solution)/shard_map/concatenate | solution.py:173
  139.0 2.5 %multiply_convert_fusion.1 = bf16[64,4096]{1,0:T(8,128)(2,1)} fusion(f32[64,4096]{1,0:T(8,128)S(1)} %mul.517, f32[64,4096]{1,0:T(8,128)} %copy.173, f32[4096]{0:T(1024)S(1)} %copy-done.35, bf16[64,4096]{1,0:T(8,128)(2,1)} %param.11), kind=kLoop, calls=%fused_computation.36 | loop fusion | flops 2359296 | bytes 3162112 | tf_op jit(solution)/shard_map/convert_element_type | solution.py:97
  (179 shorter events, 14.7 us)
Async XLA Ops:
  0.0 20.8 %copy-start.16 = (bf16[64,4608]{1,0:T(8,128)(2,1)S(1)}, bf16[64,4608]{1,0:T(8,128)(2,1)}, u32[]{:S(2)}) copy-start(bf16[64,4608]{1,0:T(8,128)(2,1)} %param.10) | copy-start | bytes 1769476
  1.0 19.8 %collective-permute-start = (bf16[3,4608]{1,0:T(4,128)(2,1)S(1)}, bf16[3,4608]{1,0:T(4,128)(2,1)S(1)}, u32[]{:S(2)}, u32[]{:S(2)}) collective-permute-start(bf16[3,4608]{1,0:T(4,128)(2,1)S(1)} %slice.290), channel_id=1, source_target_pairs={{0,1},{1,2},{2,3},{3,4},{4,5},{5,6},{6,7},{7,8},{8,9},{9,10},{10,1... | collective-permute-start | bytes 82952 | tf_op jit(solution)/shard_map/ppermute | solution.py:15
  10.0 37.5 %all-to-all-start.1 = ((f32[1,16,256]{2,0,1:T(1,128)}), f32[1,16,256]{2,0,1:T(1,128)S(1)}, u32[]{:S(2)}, u32[]{:S(2)}) async-start(f32[1,16,256]{2,0,1:T(1,128)} %broadcast_in_dim.68), calls=%async_computation.1 | async-start | bytes 32768 | tf_op jit(solution)/shard_map/all_to_all | solution.py:158
  18.5 2.5 %copy-start.34 = (f32[4608]{0:T(1024)S(1)}, f32[4608]{0:T(1024)}, u32[]{:S(2)}) copy-start(f32[4608]{0:T(1024)} %param.16) | copy-start | bytes 55300
  18.7 2.3 %copy-start.28 = (f32[64,16]{0,1:T(8,128)}, f32[64,16]{0,1:T(8,128)S(1)}, u32[]{:S(2)}) copy-start(f32[64,16]{0,1:T(8,128)S(1)} %copy.178) | copy-start | bytes 12292
  18.7 2.3 %copy-start.30 = (f32[64,16]{0,1:T(8,128)}, f32[64,16]{0,1:T(8,128)S(1)}, u32[]{:S(2)}) copy-start(f32[64,16]{0,1:T(8,128)S(1)} %copy.179) | copy-start | bytes 12292
  18.8 2.2 %copy-start.32 = (f32[64,16]{0,1:T(8,128)}, f32[64,16]{0,1:T(8,128)S(1)}, u32[]{:S(2)}) copy-start(f32[64,16]{0,1:T(8,128)S(1)} %copy.180) | copy-start | bytes 12292
  18.9 2.1 %copy-start.26 = (f32[64,16]{0,1:T(8,128)}, f32[64,16]{0,1:T(8,128)S(1)}, u32[]{:S(2)}) copy-start(f32[64,16]{0,1:T(8,128)S(1)} %copy.177) | copy-start | bytes 12292
  22.1 1.6 %copy-start.3 = (bf16[64,4608]{1,0:T(8,128)(2,1)}, bf16[64,4608]{1,0:T(8,128)(2,1)S(1)}, u32[]{:S(2)}) copy-start(bf16[64,4608]{1,0:T(8,128)(2,1)S(1)} %multiply_convert_fusion) | copy-start | bytes 1769476
  22.4 1.1 copy-start.14
  22.6 1.2 copy-start.12
  22.7 1.0 copy-start.10
  47.5 6.9 %copy-start.5 = (bf16[64,4096]{1,0:T(8,128)(2,1)S(1)}, bf16[64,4096]{1,0:T(8,128)(2,1)}, u32[]{:S(2)}) copy-start(bf16[64,4096]{1,0:T(8,128)(2,1)} %param.11) | copy-start | bytes 1572868
  47.5 29.1 %all-to-all-start = ((f32[16,1,16384]{2,1,0:T(1,128)}), f32[16,1,16384]{2,1,0:T(1,128)S(1)}, u32[]{:S(2)}, u32[]{:S(2)}) async-start(f32[16,1,16384]{2,1,0:T(1,128)} %reshape.249), calls=%async_computation | async-start | bytes 2097152 | tf_op jit(solution)/shard_map/all_to_all | solution.py:157
  55.8 20.8 %copy-start.36 = (f32[2,256]{1,0:T(2,128)}, f32[2,256]{1,0:T(2,128)S(1)}, u32[]{:S(2)}) copy-start(f32[2,256]{1,0:T(2,128)S(1)} %slice.339) | copy-start | bytes 6148
  87.9 2.7 %copy-start.2 = (f32[7,256,64]{2,1,0:T(8,128)S(1)}, f32[7,256,64]{2,1,0:T(8,128)}, u32[]{:S(2)}) copy-start(f32[7,256,64]{2,1,0:T(8,128)} %slice.351) | copy-start | bytes 1376260
  89.3 2.4 %copy-start.37 = (f32[2,256]{1,0:T(2,128)S(1)}, f32[2,256]{1,0:T(2,128)}, u32[]{:S(2)}) copy-start(f32[2,256]{1,0:T(2,128)} %copy-done.36) | copy-start | bytes 6148
  89.3 3.4 %copy-start.44 = (f32[1,256]{1,0:T(1,128)S(1)}, f32[1,256]{1,0:T(1,128)}, u32[]{:S(2)}) copy-start(f32[1,256]{1,0:T(1,128)} %slice_multiply_fusion.1) | copy-start | bytes 3076
  90.0 2.7 %copy-start.45 = (f32[1,256]{1,0:T(1,128)S(1)}, f32[1,256]{1,0:T(1,128)}, u32[]{:S(2)}) copy-start(f32[1,256]{1,0:T(1,128)} %slice.391) | copy-start | bytes 3076
  94.5 3.5 %copy-start.17 = (f32[1,256,64]{1,2,0:T(8,128)S(1)}, f32[1,256,64]{1,2,0:T(8,128)}, u32[]{:S(2)}) copy-start(f32[1,256,64]{1,2,0:T(8,128)} %slice.389) | copy-start | bytes 196612
  98.0 1.1 copy-start.18
  98.1 1.0 copy-start.7
  99.2 1.0 copy-start.4
  100.5 7.8 %copy-start.39 = (f32[64]{0:T(128)S(1)}, f32[64]{0:T(128)}, u32[]{:S(2)}) copy-start(f32[64]{0:T(128)} %param.17) | copy-start | bytes 772
  100.6 8.4 %copy-start.1 = (f32[64,4096]{1,0:T(8,128)S(1)}, f32[64,4096]{1,0:T(8,128)}, u32[]{:S(2)}) copy-start(f32[64,4096]{1,0:T(8,128)} %convert_multiply_fusion) | copy-start | bytes 3145732
  101.4 21.4 %all-to-all-start.2 = ((bf16[16,256,64]{1,2,0:T(8,128)(2,1)}), bf16[16,256,64]{1,2,0:T(8,128)(2,1)}, u32[]{:S(2)}, u32[]{:S(2)}) async-start(bf16[16,256,64]{1,2,0:T(8,128)(2,1)} %concatenate.37), calls=%async_computation.2 | async-start | bytes 1048576 | tf_op jit(solution)/shard_map/all_to_all | solution.py:162
  124.5 1.8 %copy-start.21 = (f32[64,16]{0,1:T(8,128)S(1)}, f32[64,16]{0,1:T(8,128)}, u32[]{:S(2)}) copy-start(f32[64,16]{0,1:T(8,128)} %get-tuple-element.52) | copy-start | bytes 12292
  124.7 2.6 %copy-start.20 = (f32[64,16]{0,1:T(8,128)S(1)}, f32[64,16]{0,1:T(8,128)}, u32[]{:S(2)}) copy-start(f32[64,16]{0,1:T(8,128)} %get-tuple-element.51) | copy-start | bytes 12292
  125.0 3.4 %copy-start.19 = (f32[64,16]{0,1:T(8,128)S(1)}, f32[64,16]{0,1:T(8,128)}, u32[]{:S(2)}) copy-start(f32[64,16]{0,1:T(8,128)} %get-tuple-element.54) | copy-start | bytes 12292
  126.2 3.1 %copy-start.15 = (bf16[64,1024]{0,1:T(8,128)(2,1)S(1)}, bf16[64,1024]{0,1:T(8,128)(2,1)}, u32[]{:S(2)}) copy-start(bf16[64,1024]{0,1:T(8,128)(2,1)} %copy-done.14) | copy-start | bytes 393220
  126.2 3.1 %copy-start.25 = (f32[64,64]{1,0:T(8,128)S(1)}, f32[64,64]{1,0:T(8,128)}, u32[]{:S(2)}) copy-start(f32[64,64]{1,0:T(8,128)} %fusion.73) | copy-start | bytes 49156
  126.3 3.1 %copy-start.33 = (f32[64,16]{0,1:T(8,128)S(1)}, f32[64,16]{0,1:T(8,128)}, u32[]{:S(2)}) copy-start(f32[64,16]{0,1:T(8,128)} %copy-done.32) | copy-start | bytes 12292
  126.3 3.1 %copy-start.38 = (pred[64,64]{1,0:T(8,128)(4,1)S(1)}, pred[64,64]{1,0:T(8,128)(4,1)}, u32[]{:S(2)}) copy-start(pred[64,64]{1,0:T(8,128)(4,1)} %fusion.63) | copy-start | bytes 12292
  126.3 3.1 %copy-start.43 = (f32[16,64]{1,0:T(8,128)S(1)}, f32[16,64]{1,0:T(8,128)}, u32[]{:S(2)}) copy-start(f32[16,64]{1,0:T(8,128)} %get-tuple-element.36) | copy-start | bytes 12292
  126.3 3.1 %copy-start.49 = (f32[16]{0:T(128)S(1)}, f32[16]{0:T(128)}, u32[]{:S(2)}) copy-start(f32[16]{0:T(128)} %get-tuple-element.57) | copy-start | bytes 196
  127.3 2.5 %copy-start.13 = (bf16[64,1024]{0,1:T(8,128)(2,1)S(1)}, bf16[64,1024]{0,1:T(8,128)(2,1)}, u32[]{:S(2)}) copy-start(bf16[64,1024]{0,1:T(8,128)(2,1)} %copy-done.12) | copy-start | bytes 393220
  127.3 2.5 %copy-start.24 = (f32[64,64]{1,0:T(8,128)S(1)}, f32[64,64]{1,0:T(8,128)}, u32[]{:S(2)}) copy-start(f32[64,64]{1,0:T(8,128)} %fusion.76) | copy-start | bytes 49156
  127.3 2.5 %copy-start.31 = (f32[64,16]{0,1:T(8,128)S(1)}, f32[64,16]{0,1:T(8,128)}, u32[]{:S(2)}) copy-start(f32[64,16]{0,1:T(8,128)} %copy-done.30) | copy-start | bytes 12292
  127.4 2.5 %copy-start.42 = (f32[16,64]{1,0:T(8,128)S(1)}, f32[16,64]{1,0:T(8,128)}, u32[]{:S(2)}) copy-start(f32[16,64]{1,0:T(8,128)} %get-tuple-element.35) | copy-start | bytes 12292
  127.4 2.5 %copy-start.48 = (f32[16]{0:T(128)S(1)}, f32[16]{0:T(128)}, u32[]{:S(2)}) copy-start(f32[16]{0:T(128)} %get-tuple-element.58) | copy-start | bytes 196
  129.4 1.0 copy-start.11
  129.9 1.0 copy-start.9
  129.9 1.0 copy-start.22
  129.9 1.0 copy-start.27
  129.9 1.0 copy-start.40
  129.9 0.9 copy-start.46
  135.1 2.3 %copy-start = (f32[64,64,64]{0,2,1:T(8,128)S(1)}, f32[64,64,64]{0,2,1:T(8,128)}, u32[]{:S(2)}) copy-start(f32[64,64,64]{0,2,1:T(8,128)} %get-tuple-element.13) | copy-start | bytes 3145732
  137.4 1.6 %copy-start.35 = (f32[4096]{0:T(1024)S(1)}, f32[4096]{0:T(1024)}, u32[]{:S(2)}) copy-start(f32[4096]{0:T(1024)} %param.18) | copy-start | bytes 49156
  (6 other events, 5.3 us)
where the time goes:
time: 143 us; the launch traced here: 142 us
  other arithmetic  42.4 us (30%)
  local copies, waits for them, and re-layouts  35.6 us (25%)
  waiting for transfers between devices  26.2 us (18%)
  starting transfers between devices  22.7 us (16%)
  matrix products  12.4 us (9%)
  between operations  2.27 us (2%)
    unnamed x1, other arithmetic  19.3 us
    all_to_all x1, waiting for transfers between devices, on_device(): lax.all_to_all(row_states, 'seq', split_axis=1, concat_axis=0, tiled=True)  19 us
    unnamed x114, local copies, waits for them, and re-layouts  14.4 us
    all_to_all x1, waiting for transfers between devices, on_device(): lax.all_to_all(exclusive.astype(jnp.bfloat16), 'seq', split_axis=0, conca...  7.23 us
    all_to_all x1, starting transfers between devices, on_device(): lax.all_to_all(row_pass, 'seq', split_axis=1, concat_axis=0, tiled=True)  7.22 us
    all_to_all x1, starting transfers between devices, on_device(): lax.all_to_all(exclusive.astype(jnp.bfloat16), 'seq', split_axis=0, conca...  6.93 us
    all_to_all x1, starting transfers between devices, on_device(): lax.all_to_all(row_states, 'seq', split_axis=1, concat_axis=0, tiled=True)  6.15 us
    dot_general x4, matrix products, group_terms(): jnp.einsum('tn,sn->ts', c_group, b_group, preferred_element_type=jnp.floa...  6.04 us
  transfers between devices with their start and end apart: 4, of which 2 were waited for; matrix products, arithmetic and copies ran while one was open for 33% of the time, Pallas kernels for 0%

commit v1 on v0

v1 whole, which is shorter than its diff:
```python
import functools

import jax
import jax.numpy as jnp
from jax import lax
from jax.experimental import pallas as pl
from jax.experimental.pallas import tpu as pltpu
from jax.sharding import PartitionSpec as P

GROUPS = 4
PIECES = 2
epsilon = 1e-05
f32 = jnp.float32
bf16 = jnp.bfloat16


def dot(a, b):
    return jnp.dot(a, b, preferred_element_type=f32)


def halves(v):
    high = v.astype(bf16)
    return high, (v - high.astype(f32)).astype(bf16)


def sigmoid(v):
    return 0.5 * jnp.tanh(0.5 * v) + 0.5


def kernel(
    n_seq,
    doc_ref,
    mix_ref,
    gate_ref,
    raw_ref,
    bias_ref,
    rate_ref,
    cw_ref,
    cb_ref,
    skip_ref,
    norm_ref,
    out_ref,
    pad,
    rim_out,
    rim_in,
    l_wide,
    r_wide,
    e_wide,
    pass_out,
    pass_in,
    b_end,
    score,
    c_in,
    x_s,
    xs_s,
    part_s,
    sg_s,
    a_out,
    a_in,
    ch_out,
    ch_in,
    s_out,
    s_in,
    rim_sem,
    pass_send,
    pass_recv,
    a_send,
    a_recv,
    ch_send,
    ch_recv,
    s_send,
    s_recv,
):
    rows, ch = mix_ref.shape
    inner = gate_ref.shape[1]
    heads = raw_ref.shape[1]
    head_dim = inner // heads
    state = (ch - inner) // (2 * GROUPS)
    width = inner // GROUPS
    taps = cw_ref.shape[0]
    docs = doc_ref.shape[0]
    tile = min(256, width)
    piece = width // PIECES
    span = ch // 4

    me = lax.axis_index("seq")
    r = lax.rem(me, GROUPS)
    z = me // GROUPS
    nz = n_seq // GROUPS
    slab = z * GROUPS
    others = [lax.rem(r + 2, 4), 3 - r, r + 1 - 2 * lax.rem(r, 2)]
    nxt, prv = lax.rem(me + 1, n_seq), lax.rem(me + n_seq - 1, n_seq)
    up, down = lax.rem(me + GROUPS, n_seq), lax.rem(me + n_seq - GROUPS, n_seq)

    barrier = pltpu.get_barrier_semaphore()
    near = [slab + o for o in others] + [nxt, prv, up, down]
    for d in near:
        pl.semaphore_signal(barrier, inc=1, device_id={"seq": d}, device_id_type=pl.DeviceIdType.MESH)

    def remote(src, dst, send, recv, to):
        return pltpu.make_async_remote_copy(
            src_ref=src,
            dst_ref=dst,
            send_sem=send,
            recv_sem=recv,
            device_id={"seq": to},
            device_id_type=pl.DeviceIdType.MESH,
        )

    tail = mix_ref[rows - 16 :, :].astype(f32)
    lines = [
        tail[16 - (taps - 1) + t : 16 - (taps - 1) + t + 1, i * span : (i + 1) * span]
        for t in range(taps - 1)
        for i in range(4)
    ]
    lines = lines + [jnp.zeros((16 - len(lines), span), f32)]
    rim_out[...] = jnp.concatenate(lines, axis=0).astype(bf16)
    pl.semaphore_wait(barrier, len(near))
    rim_copy = remote(rim_out, rim_in, rim_sem.at[0], rim_sem.at[1], nxt)
    rim_copy.start()

    ends = []
    total = jnp.int32(0)
    for d in range(docs):
        total = total + doc_ref[d]
        ends.append(total)

    def doc_of(pos):
        inside = jnp.zeros(pos.shape, jnp.int32)
        for end in ends:
            inside = inside + jnp.where(pos >= end, 1, 0)
        return jnp.where(pos >= 0, inside, -1)

    first = me * rows
    pos_col = first + lax.broadcasted_iota(jnp.int32, (rows, 1), 0)
    own = doc_of(pos_col)
    own_row = doc_of(first + lax.broadcasted_iota(jnp.int32, (1, rows), 1))
    prior = doc_of(jnp.full((1, 1), first - 1, jnp.int32))
    last = doc_of(jnp.full((1, 1), first + rows - 1, jnp.int32))
    tap_same = [doc_of(pos_col - (taps - 1 - t)) == own for t in range(taps - 1)]

    step = jnp.log(1.0 + jnp.exp(raw_ref[...].astype(f32) + bias_ref[...]))
    fall = -jnp.exp(rate_ref[...]) * step
    below = lax.broadcasted_iota(jnp.int32, (rows, rows), 0) >= lax.broadcasted_iota(jnp.int32, (rows, rows), 1)
    logs = jnp.dot(below.astype(f32), fall, preferred_element_type=f32, precision=lax.Precision.HIGHEST)
    l_small = jnp.exp(logs)
    r_small = jnp.exp(-logs) * step
    e_small = l_small[rows - 1 : rows, :]
    p_small = jnp.where(last == prior, e_small, 0.0)

    low8 = jnp.concatenate([e_small, p_small, skip_ref[...], jnp.zeros((5, heads), f32)], axis=0)
    stack = jnp.concatenate([l_small, r_small, low8, jnp.zeros((8, heads), f32)], axis=0)
    high = stack.astype(bf16)
    rest = stack - high.astype(f32)
    mid = rest.astype(bf16)
    lows = (rest - mid.astype(f32)).astype(bf16)
    gap = lax.broadcasted_iota(jnp.int32, (heads, tile), 0) - (
        lax.broadcasted_iota(jnp.int32, (heads, tile), 1) // head_dim
    )
    for c in range(inner // tile):
        spread = jnp.where(gap == c * (tile // head_dim), 1.0, 0.0).astype(bf16)
        wide = dot(high, spread) + dot(mid, spread) + dot(lows, spread)
        cols = slice(c * tile, (c + 1) * tile)
        l_wide[:, cols] = wide[:rows]
        r_wide[:, cols] = wide[rows : 2 * rows]
        e_wide[:, cols] = wide[2 * rows : 2 * rows + 8]

    for g in range(GROUPS):
        pass_out[g] = e_wide[:, g * width : (g + 1) * width]
    pass_copies = []
    for o in others:
        copy = remote(pass_out.at[o], pass_in.at[r], pass_send.at[o], pass_recv.at[r], slab + o)
        copy.start()
        pass_copies.append(copy)
    pass_in[r] = pass_out[r]

    pad[8:, :] = mix_ref[...].astype(f32)
    rim_copy.wait()
    rim = rim_in[...].astype(f32)
    for t in range(taps - 1):
        for i in range(4):
            row = 8 - (taps - 1) + t
            pad[row : row + 1, i * span : (i + 1) * span] = rim[t * 4 + i : t * 4 + i + 1, :]

    def conv(start, size):
        cols = pl.ds(start, size)
        acc = cb_ref[:, cols] + cw_ref[taps - 1 : taps, cols] * pad[8:, cols]
        for t in range(taps - 1):
            row = 8 - (taps - 1) + t
            acc = acc + cw_ref[t : t + 1, cols] * jnp.where(tap_same[t], pad[row : row + rows, cols], 0.0)
        return (acc * sigmoid(acc)).astype(bf16)

    bs = conv(inner, GROUPS * state)
    cs = conv(inner + GROUPS * state, GROUPS * state)
    mask = below & (own == own_row)
    to_end = own == last
    from_prior = own == prior
    for g in range(GROUPS):
        b_g = bs[:, g * state : (g + 1) * state]
        c_g = cs[:, g * state : (g + 1) * state]
        raw_score = lax.dot_general(c_g, b_g, (((1,), (1,)), ((), ())), preferred_element_type=f32)
        score[g] = jnp.where(mask, raw_score, 0.0).astype(bf16)
        c_in[g] = jnp.where(from_prior, c_g.astype(f32), 0.0).astype(bf16)
        b_end[g] = jnp.where(to_end, b_g.astype(f32), 0.0).T.astype(bf16)

    def local(g, dst):
        def body(i, _):
            at = pl.multiple_of(g * width + i * tile, tile)
            cols = pl.ds(at, tile)
            x = conv(at, tile)
            x_s[:, cols] = x
            xs = (x.astype(f32) * r_wide[:, cols]).astype(bf16)
            xs_s[:, cols] = xs
            made = dot(b_end[g], xs) * e_wide[0:1, cols]
            dst[:, pl.ds(pl.multiple_of(i * tile, tile), tile)] = made.astype(bf16)
            return 0

        lax.fori_loop(0, width // tile, body, 0)

    a_copies = []
    for o in others:
        local(o, a_out.at[o])
        copy = remote(a_out.at[o], a_in.at[r], a_send.at[o], a_recv.at[r], slab + o)
        copy.start()
        a_copies.append(copy)
    local(r, a_in.at[r])

    def inside(i, _):
        g = i // (width // tile)
        cols = pl.ds(pl.multiple_of(i * tile, tile), tile)
        part_s[:, cols] = l_wide[:, cols] * dot(score[g], xs_s[:, cols]) + e_wide[2:3, cols] * x_s[:, cols].astype(f32)
        gate = gate_ref[:, cols].astype(f32)
        sg_s[:, cols] = gate * sigmoid(gate)
        return 0

    lax.fori_loop(0, inner // tile, inside, 0)

    for o in others:
        remote(pass_out.at[o], pass_in.at[o], pass_send.at[o], pass_recv.at[o], slab + o).wait_recv()
        remote(a_out.at[o], a_in.at[o], a_send.at[o], a_recv.at[o], slab + o).wait_recv()

    for p in range(PIECES):
        cols = slice(p * piece, (p + 1) * piece)
        chain = remote(ch_out.at[p], ch_in.at[p], ch_send.at[p], ch_recv.at[p], up)

        @pl.when(z == 0)
        def _():
            ch_in[p] = jnp.zeros((state, piece), bf16)

        @pl.when(z > 0)
        def _():
            chain.wait_recv()

        held = ch_in[p].astype(f32)
        steps = []
        for k in range(GROUPS):
            steps.append(held)
            held = held * pass_in[k, 1:2, cols] + a_in[k, :, cols].astype(f32)
        ch_out[p] = held.astype(bf16)

        @pl.when(z < nz - 1)
        def _():
            chain.start()

        for k in range(GROUPS):
            s_out[k, p] = steps[k].astype(bf16)
        for o in others:
            remote(
                s_out.at[o, p], s_in.at[r, p], s_send.at[o * PIECES + p], s_recv.at[r * PIECES + p], slab + o
            ).start()
        s_in[r, p] = s_out[r, p]

    ones = jnp.where(
        lax.broadcasted_iota(jnp.int32, (tile, tile), 0) // head_dim
        == lax.broadcasted_iota(jnp.int32, (tile, tile), 1) // head_dim,
        1.0 / head_dim,
        0.0,
    ).astype(bf16)

    def finish(g, p):
        def body(i, _):
            cols = pl.ds(pl.multiple_of(g * width + p * piece + i * tile, tile), tile)
            arrived = s_in[g, p, :, pl.ds(pl.multiple_of(i * tile, tile), tile)]
            both = part_s[:, cols] + l_wide[:, cols] * dot(c_in[g], arrived)
            gated = both * sg_s[:, cols]
            sq_high, sq_low = halves(gated * gated)
            mean = dot(sq_high, ones) + dot(sq_low, ones)
            out_ref[:, cols] = (gated * lax.rsqrt(mean + epsilon) * norm_ref[:, cols]).astype(bf16)
            return 0

        lax.fori_loop(0, piece // tile, body, 0)

    for p in range(PIECES):
        finish(r, p)
        for o in [others[2], others[0], others[1]]:
            remote(
                s_out.at[o, p], s_in.at[o, p], s_send.at[o * PIECES + p], s_recv.at[o * PIECES + p], slab + o
            ).wait_recv()
            finish(o, p)

    for copy in pass_copies + a_copies:
        copy.wait_send()
    for p in range(PIECES):
        for o in others:
            remote(
                s_out.at[o, p], s_in.at[r, p], s_send.at[o * PIECES + p], s_recv.at[r * PIECES + p], slab + o
            ).wait_send()

        @pl.when(z < nz - 1)
        def _():
            remote(ch_out.at[p], ch_in.at[p], ch_send.at[p], ch_recv.at[p], up).wait_send()


def on_device(
    n_seq,
    mixer_in,
    gate_in,
    step_raw,
    step_bias,
    rate_log,
    conv_weight,
    conv_bias,
    skip_gain,
    norm_gain,
    doc_lengths,
):
    rows, ch = mixer_in.shape
    inner = gate_in.shape[1]
    heads = step_raw.shape[1]
    state = (ch - inner) // (2 * GROUPS)
    width = inner // GROUPS
    piece = width // PIECES
    vmem = pl.BlockSpec(memory_space=pltpu.VMEM)
    dma = pltpu.SemaphoreType.DMA
    return pl.pallas_call(
        functools.partial(kernel, n_seq),
        out_shape=jax.ShapeDtypeStruct((rows, inner), bf16),
        in_specs=[pl.BlockSpec(memory_space=pltpu.SMEM)] + [vmem] * 9,
        out_specs=vmem,
        scratch_shapes=[
            pltpu.VMEM((rows + 8, ch), f32),
            pltpu.VMEM((16, ch // 4), bf16),
            pltpu.VMEM((16, ch // 4), bf16),
            pltpu.VMEM((rows, inner), f32),
            pltpu.VMEM((rows, inner), f32),
            pltpu.VMEM((8, inner), f32),
            pltpu.VMEM((GROUPS, 8, width), f32),
            pltpu.VMEM((GROUPS, 8, width), f32),
            pltpu.VMEM((GROUPS, state, rows), bf16),
            pltpu.VMEM((GROUPS, rows, rows), bf16),
            pltpu.VMEM((GROUPS, rows, state), bf16),
            pltpu.VMEM((rows, inner), bf16),
            pltpu.VMEM((rows, inner), bf16),
            pltpu.VMEM((rows, inner), f32),
            pltpu.VMEM((rows, inner), f32),
            pltpu.VMEM((GROUPS, state, width), bf16),
            pltpu.VMEM((GROUPS, state, width), bf16),
            pltpu.VMEM((PIECES, state, piece), bf16),
            pltpu.VMEM((PIECES, state, piece), bf16),
            pltpu.VMEM((GROUPS, PIECES, state, piece), bf16),
            pltpu.VMEM((GROUPS, PIECES, state, piece), bf16),
            dma((2,)),
            dma((GROUPS,)),
            dma((GROUPS,)),
            dma((GROUPS,)),
            dma((GROUPS,)),
            dma((PIECES,)),
            dma((PIECES,)),
            dma((GROUPS * PIECES,)),
            dma((GROUPS * PIECES,)),
        ],
        compiler_params=pltpu.CompilerParams(
            collective_id=0, has_side_effects=True, vmem_limit_bytes=40 * 1024 * 1024
        ),
        cost_estimate=pl.CostEstimate(flops=100_000_000, bytes_accessed=2_000_000, transcendentals=1_000_000),
    )(
        doc_lengths,
        mixer_in,
        gate_in,
        step_raw,
        step_bias[None, :],
        rate_log[None, :],
        conv_weight,
        conv_bias[None, :],
        skip_gain[None, :],
        norm_gain[None, :],
    )


def solution(mesh):
    return jax.shard_map(
        functools.partial(on_device, mesh.shape["seq"]),
        mesh=mesh,
        in_specs=(
            P(("groups", "seq"), None),
            P(("groups", "seq"), None),
            P(("groups", "seq"), None),
            P(),
            P(),
            P(),
            P(),
            P(),
            P(),
            P("groups"),
        ),
        out_specs=P(("groups", "seq"), None),
        check_vma=False,
    )
```

time: 143 us -> 37 us (0.26)
  the two profiles are of different devices: /device:TPU:0 before, /device:TPU:31 now
where the time goes in v1:
time: 37 us; the launch traced here: 36.7 us
  Pallas kernels  32 us (86%)
  local copies, waits for them, and re-layouts  4.6 us (12%)
    pallas_call x1, Pallas kernels, on_device(): pl.pallas_call(functools.partial(kernel, n_seq), out_shape=jax.ShapeDtype...  32 us
    unnamed x19, local copies, waits for them, and re-layouts  3.8 us
    broadcast_in_dim x1, local copies, waits for them, and re-layouts, on_device(): conv_bias[None, :]  0.8 us

profile of v1, /device:TPU:31, one launch (start us, length us, event | category | flops | bytes accessed | tf_op | source)
XLA Modules:
  0.0 36.7 jit_solution(12064109794872041157)
XLA Ops:
  0.0 0.0 copy-start.3
  0.0 0.0 copy-start.4
  0.0 0.0 copy-start.5
  0.0 0.0 copy-start.6
  0.0 0.0 copy-start.7
  0.0 0.0 copy-start.8
  0.0 0.8 %broadcast_in_dim.17.cb_ref = f32[1,4608]{1,0:T(1,128)S(1)} reshape(f32[4608]{0:T(1024)} %param.16) | data formatting | bytes 36864 | tf_op jit(solution)/shard_map/broadcast_in_dim | solution.py:384
  0.8 0.0 copy-done.3
  0.8 0.0 copy-done.4
  0.9 0.0 copy-done.5
  0.9 0.0 copy-done.6
  0.9 0.0 copy-done.7
  0.9 0.0 copy-done.8
  0.9 0.0 copy-start
  0.9 1.1 %copy-done = bf16[64,4608]{1,0:T(8,128)(2,1)S(1)} copy-done((bf16[64,4608]{1,0:T(8,128)(2,1)S(1)}, bf16[64,4608]{1,0:T(8,128)(2,1)}, u32[]{:S(2)}) %copy-start) | copy-done | bytes 589848
  2.0 0.0 copy-start.1
  2.0 1.0 %copy-done.1 = bf16[64,4096]{1,0:T(8,128)(2,1)S(1)} copy-done((bf16[64,4096]{1,0:T(8,128)(2,1)S(1)}, bf16[64,4096]{1,0:T(8,128)(2,1)}, u32[]{:S(2)}) %copy-start.1) | copy-done | bytes 524312
  3.0 0.0 copy-start.2
  3.0 0.9 %copy-done.2 = f32[4,4608]{1,0:T(4,128)S(1)} copy-done((f32[4,4608]{1,0:T(4,128)S(1)}, f32[4,4608]{1,0:T(4,128)}, u32[]{:S(2)}) %copy-start.2) | copy-done | bytes 73752
  3.9 32.0 %shard_map.100 = bf16[64,4096]{1,0:T(8,128)(2,1)S(1)} custom-call(s32[6]{0:T(128)S(1)} %copy-done.5, bf16[64,4608]{1,0:T(8,128)(2,1)S(1)} %copy-done, bf16[64,4096]{1,0:T(8,128)(2,1)S(1)} %copy-done.1, bf16[64,64]{1,0:T(8,128)(2,1)S(1)} %copy-done.3, f32[1,64]{1,0:T(1,128)S(1)} %bitcast.5, f32[1,64]{1,0:T(1,128)S(1)} %bitcast.6, f32[4,4608]{1,0:T(4,128)S(1)} %copy-done.2, ...), custom_call_target="tpu_custom_call" | custom-call | flops 100000000 | bytes 2000000 | tf_op jit(solution)/shard_map/pallas_call | solution.py:335
  35.9 0.8 %copy.12 = bf16[64,4096]{1,0:T(8,128)(2,1)} copy(bf16[64,4096]{1,0:T(8,128)(2,1)S(1)} %shard_map.100) | data formatting | bytes 1048576
Async XLA Ops:
  0.0 0.8 %copy-start.3 = (bf16[64,64]{1,0:T(8,128)(2,1)S(1)}, bf16[64,64]{1,0:T(8,128)(2,1)}, u32[]{:S(2)}) copy-start(bf16[64,64]{1,0:T(8,128)(2,1)} %raw_ref.1) | copy-start | bytes 24580
  0.0 0.8 %copy-start.4 = (f32[4096]{0:T(1024)S(1)}, f32[4096]{0:T(1024)}, u32[]{:S(2)}) copy-start(f32[4096]{0:T(1024)} %param.18) | copy-start | bytes 49156
  0.0 0.9 %copy-start.5 = (s32[6]{0:T(128)S(1)}, s32[6]{0:T(128)}, u32[]{:S(2)}) copy-start(s32[6]{0:T(128)} %doc_ref.1) | copy-start | bytes 76
  0.0 0.9 %copy-start.6 = (f32[64]{0:T(128)S(1)}, f32[64]{0:T(128)}, u32[]{:S(2)}) copy-start(f32[64]{0:T(128)} %param.13) | copy-start | bytes 772
  0.0 0.9 %copy-start.7 = (f32[64]{0:T(128)S(1)}, f32[64]{0:T(128)}, u32[]{:S(2)}) copy-start(f32[64]{0:T(128)} %param.14) | copy-start | bytes 772
  0.0 0.9 %copy-start.8 = (f32[64]{0:T(128)S(1)}, f32[64]{0:T(128)}, u32[]{:S(2)}) copy-start(f32[64]{0:T(128)} %param.17) | copy-start | bytes 772
  0.9 1.1 %copy-start = (bf16[64,4608]{1,0:T(8,128)(2,1)S(1)}, bf16[64,4608]{1,0:T(8,128)(2,1)}, u32[]{:S(2)}) copy-start(bf16[64,4608]{1,0:T(8,128)(2,1)} %mix_ref.1) | copy-start | bytes 1769476
  2.0 1.0 %copy-start.1 = (bf16[64,4096]{1,0:T(8,128)(2,1)S(1)}, bf16[64,4096]{1,0:T(8,128)(2,1)}, u32[]{:S(2)}) copy-start(bf16[64,4096]{1,0:T(8,128)(2,1)} %gate_ref.1) | copy-start | bytes 1572868
  3.0 0.9 %copy-start.2 = (f32[4,4608]{1,0:T(4,128)S(1)}, f32[4,4608]{1,0:T(4,128)}, u32[]{:S(2)}) copy-start(f32[4,4608]{1,0:T(4,128)} %cw_ref.1) | copy-start | bytes 221188

commit v2 on v1

--- a/solution.py
+++ b/solution.py
@@ -25,6 +25,10 @@
 
 def sigmoid(v):
     return 0.5 * jnp.tanh(0.5 * v) + 0.5
+
+
+def nz_half(n_seq):
+    return max(1, n_seq // GROUPS // 2)
 
 
 def kernel(
@@ -40,9 +44,10 @@
     skip_ref,
     norm_ref,
     out_ref,
-    pad,
-    rim_out,
-    rim_in,
+    ext,
+    gate_s,
+    cw_s,
+    cb_s,
     l_wide,
     r_wide,
     e_wide,
@@ -61,6 +66,7 @@
     ch_in,
     s_out,
     s_in,
+    load_sem,
     rim_sem,
     pass_send,
     pass_recv,
@@ -81,7 +87,7 @@
     docs = doc_ref.shape[0]
     tile = min(256, width)
     piece = width // PIECES
-    span = ch // 4
+    reach = nz_half(n_seq)
 
     me = lax.axis_index("seq")
     r = lax.rem(me, GROUPS)
@@ -92,6 +98,14 @@
     nxt, prv = lax.rem(me + 1, n_seq), lax.rem(me + n_seq - 1, n_seq)
     up, down = lax.rem(me + GROUPS, n_seq), lax.rem(me + n_seq - GROUPS, n_seq)
 
+    loads = [
+        pltpu.make_async_copy(mix_ref, ext.at[pl.ds(0, rows)], load_sem.at[0]),
+        pltpu.make_async_copy(cw_ref, cw_s, load_sem.at[1]),
+        pltpu.make_async_copy(cb_ref, cb_s.at[0], load_sem.at[2]),
+        pltpu.make_async_copy(gate_ref, gate_s, load_sem.at[3]),
+    ]
+    for load in loads:
+        load.start()
     barrier = pltpu.get_barrier_semaphore()
     near = [slab + o for o in others] + [nxt, prv, up, down]
     for d in near:
@@ -107,16 +121,11 @@
             device_id_type=pl.DeviceIdType.MESH,
         )
 
-    tail = mix_ref[rows - 16 :, :].astype(f32)
-    lines = [
-        tail[16 - (taps - 1) + t : 16 - (taps - 1) + t + 1, i * span : (i + 1) * span]
-        for t in range(taps - 1)
-        for i in range(4)
-    ]
-    lines = lines + [jnp.zeros((16 - len(lines), span), f32)]
-    rim_out[...] = jnp.concatenate(lines, axis=0).astype(bf16)
     pl.semaphore_wait(barrier, len(near))
-    rim_copy = remote(rim_out, rim_in, rim_sem.at[0], rim_sem.at[1], nxt)
+    loads[0].wait()
+    rim_copy = remote(
+        ext.at[pl.ds(rows - 16, 16)], ext.at[pl.ds(rows, 16)], rim_sem.at[0], rim_sem.at[1], nxt
+    )
     rim_copy.start()
 
     ends = []
@@ -150,16 +159,12 @@
 
     low8 = jnp.concatenate([e_small, p_small, skip_ref[...], jnp.zeros((5, heads), f32)], axis=0)
     stack = jnp.concatenate([l_small, r_small, low8, jnp.zeros((8, heads), f32)], axis=0)
-    high = stack.astype(bf16)
-    rest = stack - high.astype(f32)
-    mid = rest.astype(bf16)
-    lows = (rest - mid.astype(f32)).astype(bf16)
-    gap = lax.broadcasted_iota(jnp.int32, (heads, tile), 0) - (
-        lax.broadcasted_iota(jnp.int32, (heads, tile), 1) // head_dim
+    split = jnp.concatenate(halves(stack), axis=1)
+    gap = lax.rem(lax.broadcasted_iota(jnp.int32, (2 * heads, tile), 0), heads) - (
+        lax.broadcasted_iota(jnp.int32, (2 * heads, tile), 1) // head_dim
     )
     for c in range(inner // tile):
-        spread = jnp.where(gap == c * (tile // head_dim), 1.0, 0.0).astype(bf16)
-        wide = dot(high, spread) + dot(mid, spread) + dot(lows, spread)
+        wide = dot(split, jnp.where(gap == c * (tile // head_dim), 1.0, 0.0).astype(bf16))
         cols = slice(c * tile, (c + 1) * tile)
         l_wide[:, cols] = wide[:rows]
         r_wide[:, cols] = wide[rows : 2 * rows]
@@ -174,20 +179,22 @@
         pass_copies.append(copy)
     pass_in[r] = pass_out[r]
 
-    pad[8:, :] = mix_ref[...].astype(f32)
+    place = lax.broadcasted_iota(jnp.int32, (rows, rows + 16), 1)
+    place = jnp.where(place < rows, place, place - (rows + 16))
+    behind = lax.broadcasted_iota(jnp.int32, (rows, rows + 16), 0) - place
+    shift = jnp.concatenate(
+        [jnp.where((behind == taps - 1 - t) & tap_same[t], 1.0, 0.0) for t in range(taps - 1)], axis=0
+    ).astype(bf16)
+    loads[1].wait()
+    loads[2].wait()
     rim_copy.wait()
-    rim = rim_in[...].astype(f32)
-    for t in range(taps - 1):
-        for i in range(4):
-            row = 8 - (taps - 1) + t
-            pad[row : row + 1, i * span : (i + 1) * span] = rim[t * 4 + i : t * 4 + i + 1, :]
 
     def conv(start, size):
         cols = pl.ds(start, size)
-        acc = cb_ref[:, cols] + cw_ref[taps - 1 : taps, cols] * pad[8:, cols]
+        moved = dot(shift, ext[:, cols])
+        acc = cb_s[:, cols] + cw_s[taps - 1 : taps, cols] * ext[:rows, cols].astype(f32)
         for t in range(taps - 1):
-            row = 8 - (taps - 1) + t
-            acc = acc + cw_ref[t : t + 1, cols] * jnp.where(tap_same[t], pad[row : row + rows, cols], 0.0)
+            acc = acc + cw_s[t : t + 1, cols] * moved[t * rows : (t + 1) * rows]
         return (acc * sigmoid(acc)).astype(bf16)
 
     bs = conv(inner, GROUPS * state)
@@ -215,7 +222,7 @@
             dst[:, pl.ds(pl.multiple_of(i * tile, tile), tile)] = made.astype(bf16)
             return 0
 
-        lax.fori_loop(0, width // tile, body, 0)
+        lax.fori_loop(0, width // tile, body, 0, unroll=True)
 
     a_copies = []
     for o in others:
@@ -229,41 +236,67 @@
         g = i // (width // tile)
         cols = pl.ds(pl.multiple_of(i * tile, tile), tile)
         part_s[:, cols] = l_wide[:, cols] * dot(score[g], xs_s[:, cols]) + e_wide[2:3, cols] * x_s[:, cols].astype(f32)
-        gate = gate_ref[:, cols].astype(f32)
+        gate = gate_s[:, cols].astype(f32)
         sg_s[:, cols] = gate * sigmoid(gate)
         return 0
 
-    lax.fori_loop(0, inner // tile, inside, 0)
+    loads[3].wait()
+    lax.fori_loop(0, inner // tile, inside, 0, unroll=True)
 
     for o in others:
         remote(pass_out.at[o], pass_in.at[o], pass_send.at[o], pass_recv.at[o], slab + o).wait_recv()
         remote(a_out.at[o], a_in.at[o], a_send.at[o], a_recv.at[o], slab + o).wait_recv()
 
-    for p in range(PIECES):
+    def chain(i, p):
+        at = i * PIECES + p
+        return remote(ch_out.at[at], ch_in.at[at], ch_send.at[at], ch_recv.at[at], up)
+
+    def emit(p):
         cols = slice(p * piece, (p + 1) * piece)
-        chain = remote(ch_out.at[p], ch_in.at[p], ch_send.at[p], ch_recv.at[p], up)
-
+        total = a_in[0, :, cols].astype(f32)
+        for k in range(1, GROUPS):
+            total = total * pass_in[k, 1:2, cols] + a_in[k, :, cols].astype(f32)
+        ch_out[p] = total.astype(bf16)
+
+        @pl.when(z < nz - 1)
+        def _():
+            chain(0, p).start()
+
+    def gather(i, p):
         @pl.when(z == 0)
         def _():
-            ch_in[p] = jnp.zeros((state, piece), bf16)
+            ch_in[i * PIECES + p] = jnp.zeros((state, piece), bf16)
 
         @pl.when(z > 0)
         def _():
-            chain.wait_recv()
-
+            chain(i, p).wait_recv()
+
+        if i + 1 < reach:
+            cols = slice(p * piece, (p + 1) * piece)
+            whole = pass_in[0, 1:2, cols]
+            for k in range(1, GROUPS):
+                whole = whole * pass_in[k, 1:2, cols]
+            ch_out[(i + 1) * PIECES + p] = (ch_in[i * PIECES + p].astype(f32) * whole).astype(bf16)
+
+            @pl.when(z < nz - 1)
+            def _():
+                chain(i + 1, p).start()
+
+    for p in range(PIECES):
+        emit(p)
+    for i in range(reach - 1):
+        for p in range(PIECES):
+            gather(i, p)
+    for p in range(PIECES):
+        gather(reach - 1, p)
+        cols = slice(p * piece, (p + 1) * piece)
         held = ch_in[p].astype(f32)
-        steps = []
+        for i in range(1, reach):
+            held = held + ch_in[i * PIECES + p].astype(f32)
         for k in range(GROUPS):
-            steps.append(held)
-            held = held * pass_in[k, 1:2, cols] + a_in[k, :, cols].astype(f32)
-        ch_out[p] = held.astype(bf16)
-
-        @pl.when(z < nz - 1)
-        def _():
-            chain.start()
-
-        for k in range(GROUPS):
-            s_out[k, p] = steps[k].astype(bf16)
+            s_out[k, p] = held.astype(bf16)
+            if k + 1 < GROUPS:
+                held = held * pass_in[k, 1:2, cols] + a_in[k, :, cols].astype(f32)
         for o in others:
             remote(
                 s_out.at[o, p], s_in.at[r, p], s_send.at[o * PIECES + p], s_recv.at[r * PIECES + p], slab + o
@@ -283,12 +316,11 @@
             arrived = s_in[g, p, :, pl.ds(pl.multiple_of(i * tile, tile), tile)]
             both = part_s[:, cols] + l_wide[:, cols] * dot(c_in[g], arrived)
             gated = both * sg_s[:, cols]
-            sq_high, sq_low = halves(gated * gated)
-            mean = dot(sq_high, ones) + dot(sq_low, ones)
+            mean = dot((gated * gated).astype(bf16), ones)
             out_ref[:, cols] = (gated * lax.rsqrt(mean + epsilon) * norm_ref[:, cols]).astype(bf16)
             return 0
 
-        lax.fori_loop(0, piece // tile, body, 0)
+        lax.fori_loop(0, piece // tile, body, 0, unroll=True)
 
     for p in range(PIECES):
         finish(r, p)
@@ -306,9 +338,11 @@
                 s_out.at[o, p], s_in.at[r, p], s_send.at[o * PIECES + p], s_recv.at[r * PIECES + p], slab + o
             ).wait_send()
 
-        @pl.when(z < nz - 1)
-        def _():
-            remote(ch_out.at[p], ch_in.at[p], ch_send.at[p], ch_recv.at[p], up).wait_send()
+        for i in range(reach):
+
+            @pl.when(z < nz - 1)
+            def _():
+                chain(i, p).wait_send()
 
 
 def on_device(
@@ -331,16 +365,19 @@
     width = inner // GROUPS
     piece = width // PIECES
     vmem = pl.BlockSpec(memory_space=pltpu.VMEM)
+    hbm = pl.BlockSpec(memory_space=pltpu.HBM)
+    reach = nz_half(n_seq)
     dma = pltpu.SemaphoreType.DMA
     return pl.pallas_call(
         functools.partial(kernel, n_seq),
         out_shape=jax.ShapeDtypeStruct((rows, inner), bf16),
-        in_specs=[pl.BlockSpec(memory_space=pltpu.SMEM)] + [vmem] * 9,
+        in_specs=[pl.BlockSpec(memory_space=pltpu.SMEM), hbm, hbm] + [vmem] * 3 + [hbm, hbm] + [vmem] * 2,
         out_specs=vmem,
         scratch_shapes=[
-            pltpu.VMEM((rows + 8, ch), f32),
-            pltpu.VMEM((16, ch // 4), bf16),
-            pltpu.VMEM((16, ch // 4), bf16),
+            pltpu.VMEM((rows + 16, ch), bf16),
+            pltpu.VMEM((rows, inner), bf16),
+            pltpu.VMEM(conv_weight.shape, f32),
+            pltpu.VMEM((1, ch), f32),
             pltpu.VMEM((rows, inner), f32),
             pltpu.VMEM((rows, inner), f32),
             pltpu.VMEM((8, inner), f32),
@@ -355,17 +392,18 @@
             pltpu.VMEM((rows, inner), f32),
             pltpu.VMEM((GROUPS, state, width), bf16),
             pltpu.VMEM((GROUPS, state, width), bf16),
-            pltpu.VMEM((PIECES, state, piece), bf16),
-            pltpu.VMEM((PIECES, state, piece), bf16),
+            pltpu.VMEM((reach * PIECES, state, piece), bf16),
+            pltpu.VMEM((reach * PIECES, state, piece), bf16),
             pltpu.VMEM((GROUPS, PIECES, state, piece), bf16),
             pltpu.VMEM((GROUPS, PIECES, state, piece), bf16),
+            dma((4,)),
             dma((2,)),
             dma((GROUPS,)),
             dma((GROUPS,)),
             dma((GROUPS,)),
             dma((GROUPS,)),
-            dma((PIECES,)),
-            dma((PIECES,)),
+            dma((reach * PIECES,)),
+            dma((reach * PIECES,)),
             dma((GROUPS * PIECES,)),
             dma((GROUPS * PIECES,)),
         ],
@@ -381,7 +419,7 @@
         step_bias[None, :],
         rate_log[None, :],
         conv_weight,
-        conv_bias[None, :],
+        conv_bias,
         skip_gain[None, :],
         norm_gain[None, :],
     )

time: 37 us -> 35.6 us (0.962)
  the two profiles are of different devices: /device:TPU:31 before, /device:TPU:15 now
where the time goes in v2:
time: 35.6 us; the launch traced here: 35.1 us
  Pallas kernels  28.5 us (80%)
  local copies, waits for them, and re-layouts  6.63 us (19%)
    pallas_call x1, Pallas kernels, on_device(): pl.pallas_call(functools.partial(kernel, n_seq), out_shape=jax.ShapeDtype...  28.5 us
    unnamed x21, local copies, waits for them, and re-layouts  6.63 us

profile of v2, /device:TPU:15, one launch (start us, length us, event | category | flops | bytes accessed | tf_op | source)
XLA Modules:
  0.0 35.1 jit_solution(11332137787903516095)
XLA Ops:
  0.0 0.0 copy-start.9
  0.0 0.0 copy-start.6
  0.0 0.0 copy-start.7
  0.0 0.0 copy-start.8
  0.0 0.6 %copy-done.9 = f32[64]{0:T(128)S(1)} copy-done((f32[64]{0:T(128)S(1)}, f32[64]{0:T(128)}, u32[]{:S(2)}) %copy-start.9) | copy-done | bytes 280
  0.7 0.0 copy-done.6
  0.7 0.0 copy-done.7
  0.7 0.0 copy-done.8
  0.7 0.0 copy-start
  0.7 1.1 %copy-done = bf16[64,4608]{1,0:T(8,128)(2,1)S(1)} copy-done((bf16[64,4608]{1,0:T(8,128)(2,1)S(1)}, bf16[64,4608]{1,0:T(8,128)(2,1)}, u32[]{:S(2)}) %copy-start) | copy-done | bytes 589848
  1.8 0.0 copy-start.1
  1.8 1.0 %copy-done.1 = bf16[64,4096]{1,0:T(8,128)(2,1)S(1)} copy-done((bf16[64,4096]{1,0:T(8,128)(2,1)S(1)}, bf16[64,4096]{1,0:T(8,128)(2,1)}, u32[]{:S(2)}) %copy-start.1) | copy-done | bytes 524312
  2.8 0.0 copy-start.2
  2.8 0.9 %copy-done.2 = f32[4,4608]{1,0:T(4,128)S(1)} copy-done((f32[4,4608]{1,0:T(4,128)S(1)}, f32[4,4608]{1,0:T(4,128)}, u32[]{:S(2)}) %copy-start.2) | copy-done | bytes 73752
  3.7 0.0 copy-start.3
  3.7 0.7 %copy-done.3 = f32[4608]{0:T(1024)S(1)} copy-done((f32[4608]{0:T(1024)S(1)}, f32[4608]{0:T(1024)}, u32[]{:S(2)}) %copy-start.3) | copy-done | bytes 18456
  4.4 0.0 copy-start.4
  4.4 0.7 %copy-done.4 = bf16[64,64]{1,0:T(8,128)(2,1)S(1)} copy-done((bf16[64,64]{1,0:T(8,128)(2,1)S(1)}, bf16[64,64]{1,0:T(8,128)(2,1)}, u32[]{:S(2)}) %copy-start.4) | copy-done | bytes 8216
  5.1 0.0 copy-start.5
  5.1 0.7 %copy-done.5 = f32[4096]{0:T(1024)S(1)} copy-done((f32[4096]{0:T(1024)S(1)}, f32[4096]{0:T(1024)}, u32[]{:S(2)}) %copy-start.5) | copy-done | bytes 16408
  5.9 28.5 %shard_map.100 = bf16[64,4096]{1,0:T(8,128)(2,1)S(1)} custom-call(s32[6]{0:T(128)S(1)} %copy-done.6, bf16[64,4608]{1,0:T(8,128)(2,1)S(1)} %copy-done, bf16[64,4096]{1,0:T(8,128)(2,1)S(1)} %copy-done.1, bf16[64,64]{1,0:T(8,128)(2,1)S(1)} %copy-done.4, f32[1,64]{1,0:T(1,128)S(1)} %bitcast.5, f32[1,64]{1,0:T(1,128)S(1)} %bitcast.6, f32[4,4608]{1,0:T(4,128)S(1)} %copy-done.2, ...), custom_call_target="tpu_custom_call" | custom-call | flops 100000000 | bytes 2000000 | tf_op jit(solution)/shard_map/pallas_call | solution.py:371
  34.3 0.8 %copy.12 = bf16[64,4096]{1,0:T(8,128)(2,1)} copy(bf16[64,4096]{1,0:T(8,128)(2,1)S(1)} %shard_map.100) | data formatting | bytes 1048576
Async XLA Ops:
  0.0 0.7 %copy-start.9 = (f32[64]{0:T(128)S(1)}, f32[64]{0:T(128)}, u32[]{:S(2)}) copy-start(f32[64]{0:T(128)} %param.17) | copy-start | bytes 772
  0.0 0.7 %copy-start.6 = (s32[6]{0:T(128)S(1)}, s32[6]{0:T(128)}, u32[]{:S(2)}) copy-start(s32[6]{0:T(128)} %doc_ref.1) | copy-start | bytes 76
  0.0 0.7 %copy-start.7 = (f32[64]{0:T(128)S(1)}, f32[64]{0:T(128)}, u32[]{:S(2)}) copy-start(f32[64]{0:T(128)} %param.13) | copy-start | bytes 772
  0.0 0.7 %copy-start.8 = (f32[64]{0:T(128)S(1)}, f32[64]{0:T(128)}, u32[]{:S(2)}) copy-start(f32[64]{0:T(128)} %param.14) | copy-start | bytes 772
  0.7 1.1 %copy-start = (bf16[64,4608]{1,0:T(8,128)(2,1)S(1)}, bf16[64,4608]{1,0:T(8,128)(2,1)}, u32[]{:S(2)}) copy-start(bf16[64,4608]{1,0:T(8,128)(2,1)} %mix_ref.1) | copy-start | bytes 1769476
  1.8 1.0 %copy-start.1 = (bf16[64,4096]{1,0:T(8,128)(2,1)S(1)}, bf16[64,4096]{1,0:T(8,128)(2,1)}, u32[]{:S(2)}) copy-start(bf16[64,4096]{1,0:T(8,128)(2,1)} %gate_ref.1) | copy-start | bytes 1572868
  2.8 0.9 %copy-start.2 = (f32[4,4608]{1,0:T(4,128)S(1)}, f32[4,4608]{1,0:T(4,128)}, u32[]{:S(2)}) copy-start(f32[4,4608]{1,0:T(4,128)} %cw_ref.1) | copy-start | bytes 221188
  3.7 0.7 %copy-start.3 = (f32[4608]{0:T(1024)S(1)}, f32[4608]{0:T(1024)}, u32[]{:S(2)}) copy-start(f32[4608]{0:T(1024)} %cb_ref.1) | copy-start | bytes 55300
  4.4 0.7 %copy-start.4 = (bf16[64,64]{1,0:T(8,128)(2,1)S(1)}, bf16[64,64]{1,0:T(8,128)(2,1)}, u32[]{:S(2)}) copy-start(bf16[64,64]{1,0:T(8,128)(2,1)} %raw_ref.1) | copy-start | bytes 24580
  5.1 0.7 %copy-start.5 = (f32[4096]{0:T(1024)S(1)}, f32[4096]{0:T(1024)}, u32[]{:S(2)}) copy-start(f32[4096]{0:T(1024)} %param.18) | copy-start | bytes 49156

commit v3 on v2

--- a/solution.py
+++ b/solution.py
@@ -33,21 +33,27 @@
 
 def kernel(
     n_seq,
-    doc_ref,
+    doc_hbm,
     mix_ref,
     gate_ref,
-    raw_ref,
-    bias_ref,
-    rate_ref,
+    raw_hbm,
+    bias_hbm,
+    rate_hbm,
     cw_ref,
     cb_ref,
-    skip_ref,
-    norm_ref,
+    skip_hbm,
+    norm_hbm,
     out_ref,
     ext,
     gate_s,
     cw_s,
     cb_s,
+    doc_ref,
+    raw_ref,
+    bias_ref,
+    rate_ref,
+    skip_ref,
+    norm_ref,
     l_wide,
     r_wide,
     e_wide,
@@ -79,12 +85,12 @@
 ):
     rows, ch = mix_ref.shape
     inner = gate_ref.shape[1]
-    heads = raw_ref.shape[1]
+    heads = raw_hbm.shape[1]
     head_dim = inner // heads
     state = (ch - inner) // (2 * GROUPS)
     width = inner // GROUPS
     taps = cw_ref.shape[0]
-    docs = doc_ref.shape[0]
+    docs = doc_hbm.shape[0]
     tile = min(256, width)
     piece = width // PIECES
     reach = nz_half(n_seq)
@@ -103,6 +109,12 @@
         pltpu.make_async_copy(cw_ref, cw_s, load_sem.at[1]),
         pltpu.make_async_copy(cb_ref, cb_s.at[0], load_sem.at[2]),
         pltpu.make_async_copy(gate_ref, gate_s, load_sem.at[3]),
+        pltpu.make_async_copy(doc_hbm, doc_ref, load_sem.at[4]),
+        pltpu.make_async_copy(raw_hbm, raw_ref, load_sem.at[5]),
+        pltpu.make_async_copy(bias_hbm, bias_ref.at[0], load_sem.at[6]),
+        pltpu.make_async_copy(rate_hbm, rate_ref.at[0], load_sem.at[7]),
+        pltpu.make_async_copy(skip_hbm, skip_ref.at[0], load_sem.at[8]),
+        pltpu.make_async_copy(norm_hbm, norm_ref.at[0], load_sem.at[9]),
     ]
     for load in loads:
         load.start()
@@ -127,6 +139,9 @@
         ext.at[pl.ds(rows - 16, 16)], ext.at[pl.ds(rows, 16)], rim_sem.at[0], rim_sem.at[1], nxt
     )
     rim_copy.start()
+
+    for load in loads[4:]:
+        load.wait()
 
     ends = []
     total = jnp.int32(0)
@@ -371,13 +386,19 @@
     return pl.pallas_call(
         functools.partial(kernel, n_seq),
         out_shape=jax.ShapeDtypeStruct((rows, inner), bf16),
-        in_specs=[pl.BlockSpec(memory_space=pltpu.SMEM), hbm, hbm] + [vmem] * 3 + [hbm, hbm] + [vmem] * 2,
+        in_specs=[hbm] * 10,
         out_specs=vmem,
         scratch_shapes=[
             pltpu.VMEM((rows + 16, ch), bf16),
             pltpu.VMEM((rows, inner), bf16),
             pltpu.VMEM(conv_weight.shape, f32),
             pltpu.VMEM((1, ch), f32),
+            pltpu.SMEM(doc_lengths.shape, jnp.int32),
+            pltpu.VMEM(step_raw.shape, bf16),
+            pltpu.VMEM((1, heads), f32),
+            pltpu.VMEM((1, heads), f32),
+            pltpu.VMEM((1, heads), f32),
+            pltpu.VMEM((1, inner), f32),
             pltpu.VMEM((rows, inner), f32),
             pltpu.VMEM((rows, inner), f32),
             pltpu.VMEM((8, inner), f32),
@@ -396,7 +417,7 @@
             pltpu.VMEM((reach * PIECES, state, piece), bf16),
             pltpu.VMEM((GROUPS, PIECES, state, piece), bf16),
             pltpu.VMEM((GROUPS, PIECES, state, piece), bf16),
-            dma((4,)),
+            dma((10,)),
             dma((2,)),
             dma((GROUPS,)),
             dma((GROUPS,)),
@@ -408,7 +429,7 @@
             dma((GROUPS * PIECES,)),
         ],
         compiler_params=pltpu.CompilerParams(
-            collective_id=0, has_side_effects=True, vmem_limit_bytes=40 * 1024 * 1024
+            collective_id=0, has_side_effects=True, vmem_limit_bytes=62 * 1024 * 1024
         ),
         cost_estimate=pl.CostEstimate(flops=100_000_000, bytes_accessed=2_000_000, transcendentals=1_000_000),
     )(
@@ -416,12 +437,12 @@
         mixer_in,
         gate_in,
         step_raw,
-        step_bias[None, :],
-        rate_log[None, :],
+        step_bias,
+        rate_log,
         conv_weight,
         conv_bias,
-        skip_gain[None, :],
-        norm_gain[None, :],
+        skip_gain,
+        norm_gain,
     )
 
 

time: 35.6 us -> 31.3 us (0.88)
  local copies, waits for them, and re-layouts: 6.63 us -> 1.87 us
  Pallas kernels: 28.5 us -> 29.2 us
    unnamed x21 -> x1, local copies, waits for them, and re-layouts: 6.63 us -> 1.87 us
    pallas_call x1, Pallas kernels: 28.5 us -> 29.2 us  [on_device(): pl.pallas_call(functools.partial(kernel, n_seq), out_shape=jax.ShapeDtype...]
where the time goes in v3:
time: 31.3 us; the launch traced here: 31.1 us
  Pallas kernels  29.2 us (93%)
  local copies, waits for them, and re-layouts  1.87 us (6%)
    pallas_call x1, Pallas kernels, on_device(): pl.pallas_call(functools.partial(kernel, n_seq), out_shape=jax.ShapeDtype...  29.2 us
    unnamed x1, local copies, waits for them, and re-layouts  1.87 us

profile of v3, /device:TPU:15, one launch (start us, length us, event | category | flops | bytes accessed | tf_op | source)
XLA Modules:
  0.0 31.1 jit_solution(7347231538085968140)
XLA Ops:
  0.0 29.2 %shard_map.100 = bf16[64,4096]{1,0:T(8,128)(2,1)} custom-call(s32[6]{0:T(128)} %doc_hbm.1, bf16[64,4608]{1,0:T(8,128)(2,1)} %mix_ref.1, bf16[64,4096]{1,0:T(8,128)(2,1)} %gate_ref.1, bf16[64,64]{1,0:T(8,128)(2,1)} %raw_hbm.1, f32[64]{0:T(128)} %bias_hbm.1, f32[64]{0:T(128)} %rate_hbm.1, f32[4,4608]{1,0:T(4,128)} %cw_ref.1, f32[4608]{0:T(1024)} %cb_ref.1, ...), custom_call_target="tpu_custom_call" | custom-call | flops 100000000 | bytes 2000000 | tf_op jit(solution)/shard_map/pallas_call | solution.py:386
  29.2 1.9 %copy.12 = bf16[64,4096]{1,0:T(8,128)(2,1)} copy(bf16[64,4096]{1,0:T(8,128)(2,1)} %shard_map.100) | data formatting | bytes 1048576

commit v4 on v3

--- a/solution.py
+++ b/solution.py
@@ -8,7 +8,7 @@
 from jax.sharding import PartitionSpec as P
 
 GROUPS = 4
-PIECES = 2
+PIECES = 4
 epsilon = 1e-05
 f32 = jnp.float32
 bf16 = jnp.bfloat16

time: 31.3 us -> 30.7 us (0.981)
  Pallas kernels: 29.2 us -> 28.7 us
    pallas_call x1, Pallas kernels: 29.2 us -> 28.7 us  [on_device(): pl.pallas_call(functools.partial(kernel, n_seq), out_shape=jax.ShapeDtype...]
where the time goes in v4:
time: 30.7 us; the launch traced here: 30.6 us
  Pallas kernels  28.7 us (93%)
  local copies, waits for them, and re-layouts  1.87 us (6%)
    pallas_call x1, Pallas kernels, on_device(): pl.pallas_call(functools.partial(kernel, n_seq), out_shape=jax.ShapeDtype...  28.7 us
    unnamed x1, local copies, waits for them, and re-layouts  1.87 us

profile of v4, /device:TPU:15, one launch (start us, length us, event | category | flops | bytes accessed | tf_op | source)
XLA Modules:
  0.0 30.6 jit_solution(1207187512735234974)
XLA Ops:
  0.0 28.7 %shard_map.100 = bf16[64,4096]{1,0:T(8,128)(2,1)} custom-call(s32[6]{0:T(128)} %doc_hbm.1, bf16[64,4608]{1,0:T(8,128)(2,1)} %mix_ref.1, bf16[64,4096]{1,0:T(8,128)(2,1)} %gate_ref.1, bf16[64,64]{1,0:T(8,128)(2,1)} %raw_hbm.1, f32[64]{0:T(128)} %bias_hbm.1, f32[64]{0:T(128)} %rate_hbm.1, f32[4,4608]{1,0:T(4,128)} %cw_ref.1, f32[4608]{0:T(1024)} %cb_ref.1, ...), custom_call_target="tpu_custom_call" | custom-call | flops 100000000 | bytes 2000000 | tf_op jit(solution)/shard_map/pallas_call | solution.py:386
  28.7 1.9 %copy.12 = bf16[64,4096]{1,0:T(8,128)(2,1)} copy(bf16[64,4096]{1,0:T(8,128)(2,1)} %shard_map.100) | data formatting | bytes 1048576
